TPU v7x, 32 devices: a whole 2x2x4 slice. The times are simulated.
32 devices in a mesh: dp: 16 (over z, y, x), tensor: 2 (over core).
Axes of the slice: x: 2, y: 2, z: 4, core: 2. Of those that a mesh axis runs over, the one named last changes fastest.
Arguments:
- x_in: bfloat16 [8192, 768], P('dp'), may hold values from -8 to 8
- cotangent: bfloat16 [8192, 768], P('dp'), may hold values from -8 to 8
- norm_gain: float32 [768], replicated, may hold values from 0.5 to 1.5
- w_z: bfloat16 [768, 1536], P(None, 'tensor'), may hold values from -0.21875 to 0.21875
- w_x: bfloat16 [768, 1536], P(None, 'tensor'), may hold values from -0.21875 to 0.21875
- w_bc: bfloat16 [768, 256], replicated, may hold values from -0.21875 to 0.21875
- w_dt: bfloat16 [768, 24], P(None, 'tensor'), may hold values from -0.21875 to 0.21875
- conv_x: float32 [4, 1536], P(None, 'tensor'), may hold values from -3 to 3
- conv_x_bias: float32 [1536], P('tensor'), may hold values from -1.75 to 1.75
- conv_bc: float32 [4, 256], replicated, may hold values from -3 to 3
- conv_bc_bias: float32 [256], replicated, may hold values from -1.75 to 1.75
- dt_bias: float32 [24], P('tensor'), may hold values from -6 to -2
- a_log: float32 [24], P('tensor'), may hold values from 0 to 2.77
- d_skip: float32 [24], P('tensor'), may hold values from 0.5 to 1.5
- gate_norm: float32 [1536], P('tensor'), may hold values from 0.5 to 1.5
- w_out: bfloat16 [1536, 768], P('tensor'), may hold values from -0.3125 to 0.3125
Outputs:
- y_out: bfloat16 [8192, 768], P('dp', 'tensor')
- x_grad: bfloat16 [8192, 768], P('dp', 'tensor')
- norm_gain_grad: float32 [768], P('tensor')
- w_z_grad: float32 [768, 1536], P('dp', 'tensor')
- w_x_grad: float32 [768, 1536], P('dp', 'tensor')
- w_bc_grad: float32 [768, 256], P('dp')
- w_dt_grad: float32 [768, 24], P('dp', 'tensor')
- conv_x_grad: float32 [4, 1536], P(None, 'tensor')
- conv_x_bias_grad: float32 [1536], P('tensor')
- conv_bc_grad: float32 [4, 256], replicated
- conv_bc_bias_grad: float32 [256], replicated
- dt_bias_grad: float32 [24], P('tensor')
- a_log_grad: float32 [24], P('tensor')
- d_skip_grad: float32 [24], P('tensor')
- gate_norm_grad: float32 [1536], P('tensor')
- w_out_grad: float32 [1536, 768], P('tensor', 'dp')
All inputs are finite; a program needn't handle non-finite values.
Results may differ from a plain program's by a relative error of at most 0.012.
Values sent between devices are 32-bit elements; how exact they have to be, the bound alone decides.
A program may use at most 128 MiB of HBM per device.

v0:
```python
import functools

import jax
import jax.numpy as jnp
from jax import lax
from jax.experimental import pallas as pl
from jax.experimental.pallas import tpu as pltpu
from jax.sharding import PartitionSpec as P

GROUP = 256


epsilon = 1e-05
precise = lax.Precision.HIGHEST


def lead_contract(left, right):
    return lax.dot_general(
        left, right, (((0,), (0,)), ((), ())), preferred_element_type=jnp.float32
    )


def tail_contract(left, right):
    return lax.dot_general(
        left, right, (((1,), (1,)), ((), ())), preferred_element_type=jnp.float32
    )


def causal_conv(pre_conv, kernel, offset):
    taps = kernel.shape[0]
    padded = jnp.pad(pre_conv, ((taps - 1, 0), (0, 0)))
    summed = offset[None, :] + kernel[0][None, :] * padded[: pre_conv.shape[0]]
    for tap_index in range(1, taps):
        summed = (
            summed + kernel[tap_index][None, :] * padded[tap_index : tap_index + pre_conv.shape[0]]
        )
    return summed


LANES = 128


def low_dot(left, right, contract):
    return lax.dot_general(
        left.astype(jnp.bfloat16),
        right.astype(jnp.bfloat16),
        ((contract[0], contract[1]), ((), ())),
        preferred_element_type=jnp.float32,
    )


PLAIN, LEAD, TAIL = ((1,), (0,)), ((0,), (0,)), ((1,), (1,))


def shifted(rows, distance):
    if distance == 0:
        return rows
    length = rows.shape[0]
    at = lax.broadcasted_iota(jnp.int32, rows.shape, 0)
    moved = pltpu.roll(rows, distance % length, 0)
    keep = at >= distance if distance > 0 else at < length + distance
    return jnp.where(keep, moved, 0.0)


def conv_rows(pre, taps, offset):
    count = taps.shape[0]
    total = offset + taps[count - 1 : count] * pre
    for k in range(count - 1):
        total = total + taps[k : k + 1] * shifted(pre, count - 1 - k)
    return total


def pick(array, head):
    lane = lax.broadcasted_iota(jnp.int32, array.shape, 1)
    return jnp.sum(jnp.where(lane == head, array, 0.0), axis=1, keepdims=True)


def lower(size):
    return lax.broadcasted_iota(jnp.int32, (size, size), 0) >= lax.broadcasted_iota(
        jnp.int32, (size, size), 1
    )


def prepare(dt_ref, dtb_ref, alog_ref, bc_ref, cbc_ref, cbcb_ref, scratch):
    step_ref, run_ref, stept_ref, runt_ref, bc_low_ref, pair_ref = scratch
    step = dt_ref[...] + dtb_ref[...]
    step = jnp.maximum(step, 0.0) + jnp.log1p(jnp.exp(-jnp.abs(step)))
    step_ref[...] = step
    decay = step * -jnp.exp(alog_ref[...])
    u = conv_rows(bc_ref[...], cbc_ref[...], cbcb_ref[...])
    bc_low_ref[...] = (u * jax.nn.sigmoid(u)).astype(jnp.bfloat16)
    state = bc_low_ref.shape[1] // 2
    tri = lower(GROUP).astype(jnp.float32)
    for block in range(2):
        rows = slice(block * GROUP, (block + 1) * GROUP)
        run = jnp.dot(tri, decay[rows], precision=precise, preferred_element_type=jnp.float32)
        run_ref[rows, :] = run
        runt_ref[:, rows] = run.T
        stept_ref[:, rows] = step[rows].T
        pair_ref[block] = low_dot(bc_low_ref[rows, state:], bc_low_ref[rows, :state], TAIL)


def prepare_scratch(rows, width):
    return [
        pltpu.VMEM((rows, LANES), jnp.float32),
        pltpu.VMEM((rows, LANES), jnp.float32),
        pltpu.VMEM((LANES, rows), jnp.float32),
        pltpu.VMEM((LANES, rows), jnp.float32),
        pltpu.VMEM((rows, width), jnp.bfloat16),
        pltpu.VMEM((2, GROUP, GROUP), jnp.float32),
    ]


def forward_kernel(
    x_ref, cot_ref, gain_ref, wz_ref, wx_ref, wbc_ref, wdt_ref, cx_ref, cxb_ref, cbc_ref, cbcb_ref,
    dtb_ref, alog_ref, skip_ref, gnorm_ref, wout_ref,
    normed_ref, gate_ref, xpre_ref, bc_ref, dt_ref, mixed_ref, og_ref, state_ref, sums_ref,
    *scratch,
):
    step_ref, run_ref, stept_ref, runt_ref, bc_low_ref, pair_ref = scratch
    tokens = x_ref[...].astype(jnp.float32)
    inv_rms = lax.rsqrt(jnp.mean(tokens * tokens, axis=1, keepdims=True) + epsilon)
    normed_ref[...] = (tokens * inv_rms * gain_ref[...]).astype(jnp.bfloat16)
    bc_ref[...] = low_dot(normed_ref[...], wbc_ref[...], PLAIN)
    dt_ref[...] = low_dot(normed_ref[...], wdt_ref[...], PLAIN)
    prepare(dt_ref, dtb_ref, alog_ref, bc_ref, cbc_ref, cbcb_ref, scratch)
    sums_ref[...] = jnp.zeros_like(sums_ref)
    state = bc_low_ref.shape[1] // 2
    lane = lax.broadcasted_iota(jnp.int32, (1, LANES), 1)
    left = lane < LANES // 2

    def pair_step(p, carry):
        cols = pl.ds(pl.multiple_of(p * LANES, LANES), LANES)
        pre = low_dot(normed_ref[...], wx_ref[:, cols], PLAIN)
        xpre_ref[:, cols] = pre
        gate = low_dot(normed_ref[...], wz_ref[:, cols], PLAIN)
        gate_ref[:, cols] = gate
        u = conv_rows(pre, cx_ref[:, cols], cxb_ref[:, cols])
        x_low = (u * jax.nn.sigmoid(u)).astype(jnp.bfloat16)
        values = x_low.astype(jnp.float32)
        carried_state = None
        for block in range(2):
            rows = slice(block * GROUP, (block + 1) * GROUP)
            part = values[rows]
            b_rows, c_rows = bc_low_ref[rows, :state], bc_low_ref[rows, state:]
            run_cols = [pick(run_ref[rows, :], 2 * p + side) for side in range(2)]
            total = skip_ref[:, cols] * part
            for side in range(2):
                run_row = runt_ref[pl.ds(2 * p + side, 1), rows]
                step_row = stept_ref[pl.ds(2 * p + side, 1), rows]
                differ = jnp.where(lower(GROUP), run_cols[side] - run_row, -jnp.inf)
                weights = pair_ref[block] * jnp.exp(differ) * step_row
                mine = left if side == 0 else ~left
                total = total + low_dot(weights, jnp.where(mine, part, 0.0), PLAIN)
            run = jnp.where(left, run_cols[0], run_cols[1])
            if block == 0:
                step = jnp.where(
                    left, pick(step_ref[rows, :], 2 * p), pick(step_ref[rows, :], 2 * p + 1)
                )
                to_end = jnp.exp(run[GROUP - 1 :] - run) * step
                carried_state = low_dot(to_end * part, b_rows, LEAD)
                state_ref[cols, :] = carried_state
            else:
                total = total + jnp.exp(run) * low_dot(c_rows, carried_state, TAIL)
            mixed_ref[rows, cols] = total
        gated = mixed_ref[:, cols] * gate * jax.nn.sigmoid(gate)
        og = low_dot(cot_ref[...], wout_ref[cols, :], TAIL)
        og_ref[:, cols] = og
        square = jnp.sum(gated * gated, axis=1, keepdims=True)
        inner = jnp.sum(og * gnorm_ref[:, cols] * gated, axis=1, keepdims=True)
        sums_ref[...] += jnp.where(lane == 0, square, 0.0) + jnp.where(lane == 1, inner, 0.0)
        return carry

    lax.fori_loop(0, gate_ref.shape[1] // LANES, pair_step, 0)


def backward_kernel(
    total_width,
    sums_ref, gate_ref, xpre_ref, bc_ref, dt_ref, mixed_ref, og_ref, state_ref,
    wz_ref, wx_ref, wdt_ref, cx_ref, cxb_ref, cbc_ref, cbcb_ref, dtb_ref, alog_ref, skip_ref,
    gnorm_ref, wout_ref,
    gout_ref, y_ref, glow_ref, xlow_ref, dtlow_ref, bcg_ref, partial_ref, rows_ref, heads_ref,
    *scratch,
):
    step_ref, run_ref, stept_ref, runt_ref, bc_low_ref, pair_ref = scratch[:6]
    run_grad_ref, direct_ref, colt_ref, both_ref = scratch[6:]
    prepare(dt_ref, dtb_ref, alog_ref, bc_ref, cbc_ref, cbcb_ref, scratch[:6])
    for ref in (run_grad_ref, direct_ref, colt_ref, both_ref, bcg_ref, rows_ref, heads_ref):
        ref[...] = jnp.zeros_like(ref)
    state = bc_low_ref.shape[1] // 2
    lane = lax.broadcasted_iota(jnp.int32, (1, LANES), 1)
    left = lane < LANES // 2
    taps = cx_ref.shape[0]

    def split_sum(array):
        return (
            jnp.sum(jnp.where(left, array, 0.0), axis=1, keepdims=True),
            jnp.sum(jnp.where(left, 0.0, array), axis=1, keepdims=True),
        )

    def pair_step(p, carry):
        cols = pl.ds(pl.multiple_of(p * LANES, LANES), LANES)
        spread = lax.rsqrt(sums_ref[:, 0:1] / total_width + epsilon)
        row_dot = sums_ref[:, 1:2]
        gate, mixed, og = gate_ref[:, cols], mixed_ref[:, cols], og_ref[:, cols]
        sigma = jax.nn.sigmoid(gate)
        gate_act = gate * sigma
        gated = mixed * gate_act
        gout_ref[:, cols] = (gated * spread * gnorm_ref[:, cols]).astype(jnp.bfloat16)
        rows_ref[5:6, cols] = jnp.sum(og * gated * spread, axis=0, keepdims=True)
        gated_grad = spread * og * gnorm_ref[:, cols] - gated * (
            spread * spread * spread * row_dot / total_width
        )
        grad = gated_grad * gate_act
        glow_ref[:, cols] = (
            gated_grad * mixed * sigma * (1.0 + gate * (1.0 - sigma))
        ).astype(jnp.bfloat16)
        pre = xpre_ref[:, cols]
        u = conv_rows(pre, cx_ref[:, cols], cxb_ref[:, cols])
        act = jax.nn.sigmoid(u)
        values = (u * act).astype(jnp.bfloat16).astype(jnp.float32)
        rows_ref[6:7, cols] = jnp.sum(grad * values, axis=0, keepdims=True)
        kept = state_ref[cols, :]
        later = None
        pieces = [None, None]
        for block in (1, 0):
            rows = slice(block * GROUP, (block + 1) * GROUP)
            part, dy = values[rows], grad[rows]
            b_rows, c_rows = bc_low_ref[rows, :state], bc_low_ref[rows, state:]
            run_cols = [pick(run_ref[rows, :], 2 * p + side) for side in range(2)]
            run = jnp.where(left, run_cols[0], run_cols[1])
            total = skip_ref[:, cols] * dy
            run_parts, direct_parts = [], [0.0, 0.0]
            for side in range(2):
                run_row = runt_ref[pl.ds(2 * p + side, 1), rows]
                step_row = stept_ref[pl.ds(2 * p + side, 1), rows]
                decay = jnp.exp(jnp.where(lower(GROUP), run_cols[side] - run_row, -jnp.inf))
                mine = left if side == 0 else ~left
                dy_mine = jnp.where(mine, dy, 0.0)
                near = low_dot(dy_mine, part, TAIL) * decay
                direct = near * pair_ref[block]
                both_ref[block] += near * step_row
                colt_ref[pl.ds(2 * p + side, 1), rows] = jnp.sum(direct, axis=0, keepdims=True)
                run_parts.append(jnp.sum(direct * step_row, axis=1, keepdims=True))
                total = total + low_dot(pair_ref[block] * decay * step_row, dy_mine, LEAD)
            if block == 1:
                grown = jnp.exp(run) * dy
                extra = split_sum(grown * low_dot(c_rows, kept, TAIL))
                bcg_ref[rows, state:] += low_dot(grown, kept, PLAIN)
                later = low_dot(grown, c_rows, LEAD)
                run_parts = [run_parts[side] + extra[side] for side in range(2)]
            else:
                step = jnp.where(
                    left, pick(step_ref[rows, :], 2 * p), pick(step_ref[rows, :], 2 * p + 1)
                )
                fall = jnp.exp(run[GROUP - 1 :] - run)
                to_end = fall * step
                back = low_dot(b_rows, later, TAIL)
                total = total + to_end * back
                direct_parts = split_sum(fall * part * back)
                extra = split_sum(to_end * part * back)
                bcg_ref[rows, :state] += low_dot(to_end * part, later, PLAIN)
                last = lax.broadcasted_iota(jnp.int32, (GROUP, 1), 0) == GROUP - 1
                run_parts = [
                    run_parts[side]
                    - extra[side]
                    + jnp.where(last, jnp.sum(extra[side], axis=0, keepdims=True), 0.0)
                    for side in range(2)
                ]
                direct_ref[rows, :] += jnp.where(
                    lane == 2 * p, direct_parts[0], 0.0
                ) + jnp.where(lane == 2 * p + 1, direct_parts[1], 0.0)
            run_grad_ref[rows, :] += jnp.where(lane == 2 * p, run_parts[0], 0.0) + jnp.where(
                lane == 2 * p + 1, run_parts[1], 0.0
            )
            pieces[block] = total
        du = jnp.concatenate(pieces, axis=0) * act * (1.0 + u * (1.0 - act))
        rows_ref[4:5, cols] = jnp.sum(du, axis=0, keepdims=True)
        back = 0.0
        for k in range(taps):
            rows_ref[k : k + 1, cols] = jnp.sum(
                du * shifted(pre, taps - 1 - k), axis=0, keepdims=True
            )
            back = back + cx_ref[k : k + 1, cols] * shifted(du, k - taps + 1)
        xlow_ref[:, cols] = back.astype(jnp.bfloat16)
        return carry

    lax.fori_loop(0, gate_ref.shape[1] // LANES, pair_step, 0)
    rate = -jnp.exp(alog_ref[...])
    upper = lower(GROUP).astype(jnp.float32)
    for block in range(2):
        rows = slice(block * GROUP, (block + 1) * GROUP)
        b_rows, c_rows = bc_low_ref[rows, :state], bc_low_ref[rows, state:]
        bcg_ref[rows, :state] += low_dot(both_ref[block], c_rows, LEAD)
        bcg_ref[rows, state:] += low_dot(both_ref[block], b_rows, PLAIN)
        direct = colt_ref[:, rows].T
        step = step_ref[rows, :]
        run_grad = run_grad_ref[rows, :] - direct * step
        suffix = lax.dot_general(
            upper, run_grad, (LEAD, ((), ())), precision=precise, preferred_element_type=jnp.float32
        )
        sig = jax.nn.sigmoid(dt_ref[rows, :] + dtb_ref[...])
        dt_grad = (direct_ref[rows, :] + direct + rate * suffix) * sig
        dtlow_ref[rows, :] = dt_grad.astype(jnp.bfloat16)
        heads_ref[0:1, :] += jnp.sum(dt_grad, axis=0, keepdims=True)
        heads_ref[1:2, :] += rate * jnp.sum(step * suffix, axis=0, keepdims=True)
    y_ref[...] = low_dot(gout_ref[...], wout_ref[...], PLAIN)
    partial_ref[...] = (
        low_dot(glow_ref[...], wz_ref[...], TAIL)
        + low_dot(xlow_ref[...], wx_ref[...], TAIL)
        + low_dot(dtlow_ref[...], wdt_ref[...], TAIL)
    )


def local_call(body, name, outs, scratch, *operands):
    vmem = pl.BlockSpec(memory_space=pltpu.VMEM)
    return pl.pallas_call(
        body,
        out_shape=tuple(jax.ShapeDtypeStruct(shape, kind) for shape, kind in outs),
        in_specs=[vmem] * len(operands),
        out_specs=(vmem,) * len(outs),
        scratch_shapes=scratch,
        compiler_params=pltpu.CompilerParams(vmem_limit_bytes=44 * 2**20),
        name=name,
    )(*operands)


PACK_ROWS = 16


def bit_orders(levels):
    if levels == 4:
        return ((0, 1, 2, 3), (1, 0, 2, 3), (2, 3, 0, 1))
    base = tuple(range(levels))
    third = max(1, levels // 3)
    return (base, base[third:] + base[:third], base[2 * third :] + base[: 2 * third])


def reduce_kernel(
    orders, a_ref, b_ref, c_ref, pack_ref, oa_ref, ob_ref, oc_ref, opack_ref,
    ra_ref, rb_ref, rc_ref, rpack_ref, spack_ref, send_sem, recv_sem, psend_sem, precv_sem,
):
    parts, outs, lands = (a_ref, b_ref, c_ref), (oa_ref, ob_ref, oc_ref), (ra_ref, rb_ref, rc_ref)
    levels = len(orders[0])
    count = 2**levels
    sizes = [count // 2 ** (stage + 1) for stage in range(levels)]
    starts = [sum(sizes[:stage]) for stage in range(levels)]
    me = lax.axis_index("dp")

    def my_bit(bit):
        return (me // 2**bit) % 2

    def partner(bit):
        return me + (1 - 2 * my_bit(bit)) * 2**bit

    def first_chunk(order, k, kept):
        own = my_bit(order[0])
        chunk = (own if kept else 1 - own) * 2 ** order[0]
        for place in range(1, levels):
            relative = (k // 2 ** (levels - 1 - place)) % 2
            chunk = chunk + ((my_bit(order[place]) + relative + 1) % 2) * 2 ** order[place]
        return chunk

    def transfer(g, stage, k):
        if stage == 0:
            source = parts[g].at[first_chunk(orders[g], k, False)]
        else:
            source = lands[g].at[starts[stage - 1] + k]
        slot = starts[stage] + k
        return pltpu.make_async_remote_copy(
            src_ref=source,
            dst_ref=lands[g].at[slot],
            send_sem=send_sem.at[g, slot],
            recv_sem=recv_sem.at[g, slot],
            device_id={"dp": partner(orders[g][stage])},
            device_id_type=pl.DeviceIdType.MESH,
        )

    def pack_transfer(stage):
        return pltpu.make_async_remote_copy(
            src_ref=pack_ref if stage == 0 else spack_ref.at[stage - 1],
            dst_ref=rpack_ref.at[stage],
            send_sem=psend_sem.at[stage],
            recv_sem=precv_sem.at[stage],
            device_id={"dp": partner(stage)},
            device_id_type=pl.DeviceIdType.MESH,
        )

    barrier = pltpu.get_barrier_semaphore()
    for bit in range(levels):
        pl.semaphore_signal(
            barrier, inc=1, device_id={"dp": partner(bit)}, device_id_type=pl.DeviceIdType.MESH
        )
    pl.semaphore_wait(barrier, levels)

    def begin(k, carry):
        for g in range(3):
            transfer(g, 0, k).start()
        return carry

    pack_transfer(0).start()
    lax.fori_loop(0, sizes[0], begin, 0)
    for stage in range(levels):
        half = sizes[stage] // 2
        for g in range(3):

            def step(k, carry, g=g, stage=stage, forward=False):
                transfer(g, stage, k).wait_recv()
                slot = starts[stage] + k
                if stage == 0:
                    own = parts[g][first_chunk(orders[g], k, True)]
                else:
                    own = lands[g][starts[stage - 1] + sizes[stage] + k]
                total = lands[g][slot] + own
                if stage == levels - 1:
                    outs[g][...] = total
                else:
                    lands[g][slot] = total
                if forward:
                    transfer(g, stage + 1, k).start()
                return carry

            if stage < levels - 1:
                lax.fori_loop(0, half, functools.partial(step, forward=True), 0)
                lax.fori_loop(half, sizes[stage], step, 0)
            else:
                step(0, 0)
        pack_transfer(stage).wait_recv()
        before = pack_ref[...] if stage == 0 else spack_ref[stage - 1]
        pack_total = before + rpack_ref[stage]
        if stage == levels - 1:
            opack_ref[...] = pack_total
        else:
            spack_ref[stage] = pack_total
            pack_transfer(stage + 1).start()
    for stage in range(levels):
        pack_transfer(stage).wait_send()

        def finish(k, carry, stage=stage):
            for g in range(3):
                transfer(g, stage, k).wait_send()
            return carry

        lax.fori_loop(0, sizes[stage], finish, 0)


def reduce_all(a, b, c, pack):
    count, rows, width = a.shape
    levels = count.bit_length() - 1
    vmem = pl.BlockSpec(memory_space=pltpu.VMEM)
    part = jax.ShapeDtypeStruct((rows, width), jnp.float32)
    return pl.pallas_call(
        functools.partial(reduce_kernel, bit_orders(levels)),
        out_shape=(part, part, part, jax.ShapeDtypeStruct(pack.shape, jnp.float32)),
        in_specs=[vmem] * 4,
        out_specs=(vmem,) * 4,
        scratch_shapes=[pltpu.VMEM((count - 1, rows, width), jnp.float32)] * 3
        + [
            pltpu.VMEM((levels,) + pack.shape, jnp.float32),
            pltpu.VMEM((levels,) + pack.shape, jnp.float32),
            pltpu.SemaphoreType.DMA((3, count - 1)),
            pltpu.SemaphoreType.DMA((3, count - 1)),
            pltpu.SemaphoreType.DMA((levels,)),
            pltpu.SemaphoreType.DMA((levels,)),
        ],
        compiler_params=pltpu.CompilerParams(
            collective_id=0, has_side_effects=True, vmem_limit_bytes=44 * 2**20
        ),
        name="reduce_all",
    )(a, b, c, pack)


def on_device(
    x_in,
    cotangent,
    norm_gain,
    w_z,
    w_x,
    w_bc,
    w_dt,
    conv_x,
    conv_x_bias,
    conv_bc,
    conv_bc_bias,
    dt_bias,
    a_log,
    d_skip,
    gate_norm,
    w_out,
):
    row_count, model_width = x_in.shape
    pair_count = lax.axis_size("tensor")
    half_width = model_width // pair_count
    col_start = lax.axis_index("tensor") * half_width
    inner_width = w_z.shape[1]
    heads_here = dt_bias.shape[0]
    total_width = inner_width * pair_count
    tokens = x_in.astype(jnp.float32)
    inv_rms = lax.rsqrt(jnp.mean(tokens * tokens, axis=1, keepdims=True) + epsilon)
    x_hat = tokens * inv_rms
    bc_width = w_bc.shape[1]

    def head_row(vector):
        return jnp.pad(vector, (0, LANES - heads_here))[None, :]

    w_dt_padded = jnp.pad(w_dt, ((0, 0), (0, LANES - heads_here)))
    skip_row = jnp.repeat(d_skip, inner_width // heads_here)[None, :]
    wide = (row_count, inner_width)
    shared = (
        conv_x,
        conv_x_bias[None, :],
        conv_bc,
        conv_bc_bias[None, :],
        head_row(dt_bias),
        head_row(a_log),
        skip_row,
        gate_norm[None, :],
        w_out,
    )
    normed, gate_pre, x_pre, bc_pre, dt_pre, mixed_out, out_grad, states, sums = local_call(
        forward_kernel,
        "forward",
        (
            ((row_count, model_width), jnp.bfloat16),
            (wide, jnp.float32),
            (wide, jnp.float32),
            ((row_count, bc_width), jnp.float32),
            ((row_count, LANES), jnp.float32),
            (wide, jnp.float32),
            (wide, jnp.float32),
            ((inner_width, bc_width // 2), jnp.float32),
            ((row_count, LANES), jnp.float32),
        ),
        prepare_scratch(row_count, bc_width),
        x_in, cotangent, norm_gain[None, :], w_z, w_x, w_bc, w_dt_padded, *shared,
    )
    sums = lax.psum(sums, "tensor")
    gate_out, y_part, gate_low, x_pre_low, dt_padded, bc_part_grad, partial_grad, rows, heads = (
        local_call(
            functools.partial(backward_kernel, total_width),
            "backward",
            (
                (wide, jnp.bfloat16),
                ((row_count, model_width), jnp.float32),
                (wide, jnp.bfloat16),
                (wide, jnp.bfloat16),
                ((row_count, LANES), jnp.bfloat16),
                ((row_count, bc_width), jnp.float32),
                ((row_count, model_width), jnp.float32),
                ((8, inner_width), jnp.float32),
                ((8, LANES), jnp.float32),
            ),
            prepare_scratch(row_count, bc_width)
            + [
                pltpu.VMEM((row_count, LANES), jnp.float32),
                pltpu.VMEM((row_count, LANES), jnp.float32),
                pltpu.VMEM((LANES, row_count), jnp.float32),
                pltpu.VMEM((2, GROUP, GROUP), jnp.float32),
            ],
            sums, gate_pre, x_pre, bc_pre, dt_pre, mixed_out, out_grad, states,
            w_z, w_x, w_dt_padded, *shared,
        )
    )
    out_share = lax.psum_scatter(y_part, "tensor", scatter_dimension=1, tiled=True)
    token_half = lax.dynamic_slice_in_dim(tokens, col_start, half_width, 1)
    result = (token_half + out_share).astype(jnp.bfloat16)
    w_out_grad = lead_contract(cotangent, gate_out)
    bc_conv_grad = lax.psum(bc_part_grad, "tensor")
    bc_conv_back = jax.vjp(
        lambda *pieces: jax.nn.silu(causal_conv(*pieces)), bc_pre, conv_bc, conv_bc_bias
    )[1]
    bc_pre_grad, conv_bc_grad, conv_bc_bias_grad = bc_conv_back(bc_conv_grad)
    bc_pre_low = bc_pre_grad.astype(jnp.bfloat16)
    conv_taps = conv_x.shape[0]
    hat_half = lax.dynamic_slice_in_dim(x_hat, col_start, half_width, 1)
    gain_half = lax.dynamic_slice_in_dim(norm_gain, col_start, half_width, 0)
    normed_grad = lax.psum(partial_grad, "tensor") + tail_contract(bc_pre_low, w_bc)
    grad_half = lax.dynamic_slice_in_dim(normed_grad, col_start, half_width, 1)
    weighted_in = grad_half * gain_half[None, :]
    in_dot = jnp.sum(normed_grad * norm_gain[None, :] * x_hat, axis=1)
    norm_gain_grad = jnp.sum(grad_half * hat_half, axis=0)
    cot_half = lax.dynamic_slice_in_dim(cotangent, col_start, half_width, 1).astype(jnp.float32)
    x_grad = (cot_half + inv_rms * (weighted_in - hat_half * in_dot[:, None] / model_width)).astype(
        jnp.bfloat16
    )
    count = lax.axis_size("dp")
    half_bc = bc_pre_low.shape[1] // 2

    def chunks(array):
        return array.reshape(count, model_width // count, array.shape[1])

    part_a = chunks(jnp.concatenate([w_out_grad, lead_contract(normed, dt_padded)], axis=1))
    part_b = chunks(
        lead_contract(normed, jnp.concatenate([gate_low, bc_pre_low[:, :half_bc]], axis=1))
    )
    part_c = chunks(
        lead_contract(normed, jnp.concatenate([x_pre_low, bc_pre_low[:, half_bc:]], axis=1))
    )
    small = (
        rows,
        conv_bc_grad,
        conv_bc_bias_grad,
        heads[:2],
        norm_gain_grad,
    )
    flat = jnp.concatenate([array.reshape(-1) for array in small])
    pack = jnp.pad(flat, (0, PACK_ROWS * 768 - flat.shape[0])).reshape(PACK_ROWS, 768)
    sum_a, sum_b, sum_c, pack_total = reduce_all(part_a, part_b, part_c, pack)
    w_out_share = jnp.transpose(sum_a[:, :inner_width])
    w_dt_share = sum_a[:, inner_width : inner_width + heads_here]
    w_z_share = sum_b[:, :inner_width]
    w_x_share = sum_c[:, :inner_width]
    w_bc_share = jnp.concatenate([sum_b[:, inner_width:], sum_c[:, inner_width:]], axis=1)
    flat_total = pack_total.reshape(-1)
    totals, at = [], 0
    for array in small:
        totals.append(flat_total[at : at + array.size].reshape(array.shape))
        at += array.size
    rows_total, conv_bc_total, conv_bc_bias_total, heads_total, norm_gain_total = totals
    conv_x_total = rows_total[:conv_taps]
    conv_x_bias_total = rows_total[conv_taps]
    gate_norm_total = rows_total[conv_taps + 1]
    d_skip_total = jnp.sum(rows_total[conv_taps + 2].reshape(heads_here, -1), axis=1)
    dt_bias_total = heads_total[0, :heads_here]
    a_log_total = heads_total[1, :heads_here]
    return (
        result,
        x_grad,
        norm_gain_total,
        w_z_share,
        w_x_share,
        w_bc_share,
        w_dt_share,
        conv_x_total,
        conv_x_bias_total,
        conv_bc_total,
        conv_bc_bias_total,
        dt_bias_total,
        a_log_total,
        d_skip_total,
        gate_norm_total,
        w_out_share,
    )


def solution(mesh):
    in_specs = (
        P("dp", None),
        P("dp", None),
        P(),
        P(None, "tensor"),
        P(None, "tensor"),
        P(),
        P(None, "tensor"),
        P(None, "tensor"),
        P("tensor"),
        P(),
        P(),
        P("tensor"),
        P("tensor"),
        P("tensor"),
        P("tensor"),
        P("tensor", None),
    )
    out_specs = (
        P("dp", "tensor"),
        P("dp", "tensor"),
        P("tensor"),
        P("dp", "tensor"),
        P("dp", "tensor"),
        P("dp", None),
        P("dp", "tensor"),
        P(None, "tensor"),
        P("tensor"),
        P(),
        P(),
        P("tensor"),
        P("tensor"),
        P("tensor"),
        P("tensor"),
        P("tensor", "dp"),
    )
    return jax.shard_map(
        on_device, mesh=mesh, in_specs=in_specs, out_specs=out_specs, check_vma=False
    )
```

profile of v0, /device:TPU:0, one launch (start us, length us, event | category | flops | bytes accessed | tf_op | source)
XLA Modules:
  0.0 226.7 jit_solution(1971335179112901452)
XLA Ops:
  7.2 0.9 copy.32
  8.1 0.7 broadcast_in_dim.35
  9.0 0.7 broadcast_in_dim.15.cxb_ref
  9.6 0.7 broadcast_in_dim.36.gnorm_ref
  10.3 0.7 broadcast_in_dim.14.gain_ref
  11.8 1.1 copy-done
  12.9 1.1 copy-done.4
  14.0 1.3 copy-done.7
  15.3 1.3 copy-done.9
  16.6 1.3 copy-done.11
  17.8 1.0 copy-done.14
  18.8 0.7 copy-done.31
  19.5 0.7 copy-done.33
  20.9 11.0 %forward.1 = (bf16[512,768]{1,0:T(8,128)(2,1)S(1)}, f32[512,768]{1,0:T(8,128)S(1)}, f32[512,768]{1,0:T(8,128)}, f32[512,256]{1,0:T(8,128)S(1)}, f32[512,128]{1,0...) custom-call(bf16[512,768]{1,0:T(8,128)(2,1)S(1)} %copy-done, ...), custom_call_target="tpu_custom_call" | custom-call | tf_op jit(solution)/shard_map/forward/pallas_call | solution.py:317
  32.0 1.2 copy-done.17
  33.2 0.7 copy-done.22
  33.9 0.7 copy-done.24
  34.6 0.7 copy-done.27
  35.4 21.1 %all-reduce.17.cloned.1.call-done.sums_ref = f32[512,128]{1,0:T(8,128)} async-done(((f32[512,128]{1,0:T(8,128)}), f32[512,128]{1,0:T(8,128)}) %all-reduce.17.cloned.1.call-update) | async-done | bytes 262160 | tf_op jit(solution)/shard_map/psum | solution.py:537
  56.5 1.3 copy-done.10
  57.7 1.3 copy-done.12
  59.0 1.0 copy-done.23
  60.0 0.9 copy-done.25
  61.0 0.9 copy-done.26
  61.9 0.7 copy-done.36
  62.6 18.7 %backward.1 = (bf16[512,768]{1,0:T(8,128)(2,1)S(1)}, f32[512,768]{1,0:T(8,128)S(1)}, bf16[512,768]{1,0:T(8,128)(2,1)S(1)}, bf16[512,768]{1,0:T(8,128)(2,1)S(1)},...) custom-call(f32[512,128]{1,0:T(8,128)S(1)} %copy-done.26, ...), custom_call_target="tpu_custom_call" | custom-call | tf_op jit(solution)/shard_map/backward/pallas_call | solution.py:317
  81.3 0.8 copy-done.13
  82.1 1.1 copy-done.16
  83.3 0.9 copy-done.18
  84.2 0.9 copy-done.20
  85.1 0.8 copy-done.21
  88.1 0.9 copy-done.1
  88.9 1.3 convert_element_type.22
  92.6 0.8 convolution_bitcast_fusion
  93.4 1.7 pad_maximum_fusion
  95.1 2.3 %copy.33 = f32[768,896]{1,0:T(8,128)S(1)} copy(f32[768,896]{0,1:T(8,128)} %pad_maximum_fusion) | data formatting | bytes 5505024 | tf_op jit(solution)/shard_map/concatenate | solution.py:592
  97.5 1.4 constant_dynamic-update-slice_fusion.4
  98.8 11.6 %all-reduce.19.cloned.1.call-done = (f32[512,768]{1,0:T(8,128)}, f32[512,256]{1,0:T(8,128)}) async-done(((f32[512,768]{1,0:T(8,128)}, f32[512,256]{1,0:T(8,128)}), (f32[512,768]{1,0:T(8,128)}, f32[512,256]{1,0:T(8,128)})) %all-reduce.19.cloned.1.call-update) | async-done | bytes 2097168 | tf_op jit(solution)/shard_map/psum | solution.py:577
  110.4 3.5 %multiply_reduce_fusion.6 = (f32[256]{0:T(256)S(1)}, f32[256]{0:T(256)S(1)}, f32[256]{0:T(256)S(1)}, f32[256]{0:T(256)S(1)}, f32[256]{0:T(256)S(1)}, /*index=5*/f32[512,256]{1,0:T(8,128)S(1)}) fusion(f32[512,256]{1,0:T(8,128)} %copy-done.13, f32[512,256]{1,0:T(8,128)} %get-tuple-element.85, f32[256]{0:T(256)} %bitcast.44, f32[256]{0:T(256)} %bitcast.46, ...), kind=kLoop, calls=%fused_computation.24 | loop fusion | flops 3406592 | bytes 1583104 | tf_op jit(solution)/shard_map/transpose(jvp())/reduce_sum | solution.py:35
  114.0 0.9 broadcast_multiply_fusion.4
  115.1 0.9 constant_dynamic-update-slice_fusion.1
  117.7 1.0 multiply_reduce_fusion.2
  119.3 1.4 reshape.111.pack_ref
  120.8 1.1 fusion.14
  121.9 2.3 fusion.4
  124.1 1.0 fusion
  125.2 85.3 %reduce_all.1 = (f32[48,896]{1,0:T(8,128)S(1)}, f32[48,896]{1,0:T(8,128)S(1)}, f32[48,896]{1,0:T(8,128)S(1)}, f32[16,768]{1,0:T(8,128)S(1)}) custom-call(f32[16,48,896]{2,1,0:T(8,128)S(1)} %bitcast.38, f32[16,48,896]{2,1,0:T(8,128)S(1)} %bitcast.37, f32[16,48,896]{2,1,0:T(8,128)S(1)} %bitcast.36, f32[16,768]{1,0:T(8,128)S(1)} %copy-done.28), custom_call_target="tpu_custom_call" | custom-call | tf_op jit(solution)/shard_map/reduce_all/pallas_call | solution.py:452
  218.0 2.2 add_convert_fusion.1
  (113 shorter events, 16.2 us)
Async XLA Ops:
  7.2 49.3 %all-reduce.17.cloned.1.call-start = ((), (), s32[]{:S(2)}) async-start(), calls=%async_computation.1 | async-start | bytes 524288 | tf_op jit(solution)/shard_map/psum | solution.py:537
  9.6 22.3 %copy-start.35 = (f32[1,768]{1,0:T(1,128)}, f32[1,768]{1,0:T(1,128)S(1)}, u32[]{:S(2)}) copy-start(f32[1,768]{1,0:T(1,128)S(1)} %broadcast_in_dim.15.cxb_ref) | copy-start | bytes 9220
  11.7 1.1 copy-start
  12.9 1.1 copy-start.4
  14.0 1.3 copy-start.7
  15.3 1.3 copy-start.9
  16.6 1.3 copy-start.11
  17.8 1.0 copy-start.14
  18.8 0.7 copy-start.31
  19.5 0.7 copy-start.33
  20.2 0.7 copy-start.39
  20.9 35.6 %copy-start.8 = (bf16[768,768]{1,0:T(8,128)(2,1)S(1)}, bf16[768,768]{1,0:T(8,128)(2,1)}, u32[]{:S(2)}) copy-start(bf16[768,768]{1,0:T(8,128)(2,1)} %wz_ref.3) | copy-start | bytes 3538948
  20.9 35.6 %copy-start.32 = (f32[4,768]{1,0:T(4,128)S(1)}, f32[4,768]{1,0:T(4,128)}, u32[]{:S(2)}) copy-start(f32[4,768]{1,0:T(4,128)} %cx_ref.3) | copy-start | bytes 36868
  20.9 35.6 %copy-start.34 = (f32[4,256]{1,0:T(4,128)S(1)}, f32[4,256]{1,0:T(4,128)}, u32[]{:S(2)}) copy-start(f32[4,256]{1,0:T(4,128)} %cbc_ref.3) | copy-start | bytes 12292
  32.0 1.2 copy-start.17
  33.2 0.7 copy-start.22
  33.9 0.7 copy-start.24
  34.6 0.7 copy-start.27
  35.3 57.0 %copy-start.2 = (bf16[512,768]{1,0:T(8,128)(2,1)}, bf16[512,768]{1,0:T(8,128)(2,1)S(1)}, u32[]{:S(2)}) copy-start(bf16[512,768]{1,0:T(8,128)(2,1)S(1)} %get-tuple-element.50) | copy-start | bytes 2359300
  35.3 75.1 %all-reduce.19.cloned.1.call-start = ((), (), s32[]{:S(2)}) async-start(), calls=%async_computation.3 | async-start | bytes 4194304 | tf_op jit(solution)/shard_map/psum | solution.py:577
  56.5 1.3 copy-start.10
  57.7 1.3 copy-start.12
  59.0 1.0 copy-start.23
  60.0 0.9 copy-start.25
  61.0 0.9 copy-start.26
  61.9 0.7 copy-start.36
  81.3 0.8 copy-start.13
  82.1 1.1 copy-start.16
  83.3 0.9 copy-start.18
  84.2 0.9 copy-start.20
  85.1 0.8 copy-start.21
  85.9 0.7 copy-start.29
  87.8 1.1 copy-start.1
  87.8 2.4 %copy-start.45 = (f32[768]{0:T(1024)S(1)}, f32[768]{0:T(1024)}, u32[]{:S(2)}) copy-start(f32[768]{0:T(1024)} %param.18) | copy-start | bytes 9220
  87.8 130.2 %reduce-scatter.2.cloned.1.call-start = ((), (), s32[]{:S(2)}) async-start(), calls=%async_computation.2 | async-start | bytes 2359296 | tf_op jit(solution)/shard_map/reduce_scatter | solution.py:564
  88.9 2.7 %copy-start.38 = (f32[8,768]{1,0:T(8,128)S(1)}, f32[8,768]{1,0:T(8,128)}, u32[]{:S(2)}) copy-start(f32[8,768]{1,0:T(8,128)} %copy-done.37) | copy-start | bytes 73732
  88.9 3.4 %copy-start.30 = (bf16[512,128]{1,0:T(8,128)(2,1)S(1)}, bf16[512,128]{1,0:T(8,128)(2,1)}, u32[]{:S(2)}) copy-start(bf16[512,128]{1,0:T(8,128)(2,1)} %copy-done.29) | copy-start | bytes 393220
  90.2 2.4 %copy-start.5 = (bf16[512,768]{1,0:T(8,128)(2,1)S(1)}, bf16[512,768]{1,0:T(8,128)(2,1)}, u32[]{:S(2)}) copy-start(bf16[512,768]{1,0:T(8,128)(2,1)} %cot_ref.1) | copy-start | bytes 2359300
  97.4 13.0 %copy-start.40 = (f32[256]{0:T(256)S(1)}, f32[256]{0:T(256)}, u32[]{:S(2)}) copy-start(f32[256]{0:T(256)} %param.26) | copy-start | bytes 3076
  110.4 3.5 %copy-start.44 = (f32[8064]{0:T(1024)S(1)}, f32[8064]{0:T(1024)}, u32[]{:S(2)}) copy-start(f32[8064]{0:T(1024)} %constant_dynamic-update-slice_fusion.4) | copy-start | bytes 96772
  114.9 1.2 copy-start.15
  114.9 1.6 copy-start.43
  115.1 2.1 copy-start.42
  116.5 1.1 copy-start.6
  116.5 1.1 copy-start.46
  117.2 4.7 %copy-start.3 = (bf16[512,768]{1,0:T(8,128)(2,1)S(1)}, bf16[512,768]{1,0:T(8,128)(2,1)}, u32[]{:S(2)}) copy-start(bf16[512,768]{1,0:T(8,128)(2,1)} %copy-done.2) | copy-start | bytes 2359300
  121.8 2.3 %copy-start.19 = (bf16[512,768]{1,0:T(8,128)(2,1)S(1)}, bf16[512,768]{1,0:T(8,128)(2,1)}, u32[]{:S(2)}) copy-start(bf16[512,768]{1,0:T(8,128)(2,1)} %copy-done.18) | copy-start | bytes 2359300
  124.1 1.0 copy-start.28
  (2 other events, 1.2 us)
Sparse Core Ops, SparseCore 0:
  35.5 20.9 all-reduce.16
  87.9 22.4 all-reduce.18
  112.7 10.2 reduce-scatter.1
where the time goes:
time: 228 us; the launch traced here: 227 us
  Pallas kernels  115 us (50%)
  local copies, waits for them, and re-layouts  47.3 us (21%)
  waiting for transfers between devices  32.7 us (14%)
  between operations  14.1 us (6%)
  other arithmetic  12.3 us (5%)
  matrix products  5.02 us (2%)
    pallas_call x1, Pallas kernels, reduce_all(): pl.pallas_call(functools.partial(reduce_kernel, bit_orders(levels)), out_...  85.3 us
    unnamed x101, local copies, waits for them, and re-layouts  30.8 us
    pallas_call x2, Pallas kernels, local_call(): pl.pallas_call(body, out_shape=tuple((jax.ShapeDtypeStruct(shape, kind) f...  29.8 us
    psum x1, waiting for transfers between devices, on_device(): sums = lax.psum(sums, 'tensor')  21.1 us
    psum x1, waiting for transfers between devices, on_device(): lax.psum(partial_grad, 'tensor') + tail_contract(bc_pre_low, w_bc)  11.6 us
  transfers between devices with their start and end apart: 3, of which 2 were waited for; matrix products, arithmetic and copies ran while one was open for 14% of the time, Pallas kernels for 38%

commit v1 on v0

--- a/solution.py
+++ b/solution.py
@@ -470,6 +470,64 @@
     )(a, b, c, pack)
 
 
+def pair_kernel(halved, *refs):
+    count = len(halved)
+    sources, outs, lands = refs[:count], refs[count : 2 * count], refs[2 * count : 3 * count]
+    send_sem, recv_sem = refs[3 * count :]
+    me = lax.axis_index("tensor")
+    other = 1 - me
+
+    def view(i, owner):
+        if not halved[i]:
+            return sources[i]
+        width = outs[i].shape[1]
+        return sources[i].at[:, pl.ds(pl.multiple_of(owner * width, LANES), width)]
+
+    barrier = pltpu.get_barrier_semaphore()
+    pl.semaphore_signal(
+        barrier, inc=1, device_id={"tensor": other}, device_id_type=pl.DeviceIdType.MESH
+    )
+    pl.semaphore_wait(barrier, 1)
+    copies = [
+        pltpu.make_async_remote_copy(
+            src_ref=view(i, other),
+            dst_ref=lands[i],
+            send_sem=send_sem.at[i],
+            recv_sem=recv_sem.at[i],
+            device_id={"tensor": other},
+            device_id_type=pl.DeviceIdType.MESH,
+        )
+        for i in range(count)
+    ]
+    for copy in copies:
+        copy.start()
+    for i in range(count):
+        copies[i].wait_recv()
+        outs[i][...] = view(i, me)[...] + lands[i][...]
+    for copy in copies:
+        copy.wait_send()
+
+
+def pair_sum(arrays, halved, number):
+    vmem = pl.BlockSpec(memory_space=pltpu.VMEM)
+    shapes = [
+        (array.shape[0], array.shape[1] // 2 if half else array.shape[1])
+        for array, half in zip(arrays, halved)
+    ]
+    return pl.pallas_call(
+        functools.partial(pair_kernel, halved),
+        out_shape=tuple(jax.ShapeDtypeStruct(shape, jnp.float32) for shape in shapes),
+        in_specs=[vmem] * len(arrays),
+        out_specs=(vmem,) * len(arrays),
+        scratch_shapes=[pltpu.VMEM(shape, jnp.float32) for shape in shapes]
+        + [pltpu.SemaphoreType.DMA((len(arrays),))] * 2,
+        compiler_params=pltpu.CompilerParams(
+            collective_id=number, has_side_effects=True, vmem_limit_bytes=24 * 2**20
+        ),
+        name="pair_sum",
+    )(*arrays)
+
+
 def on_device(
     x_in,
     cotangent,
@@ -534,7 +592,7 @@
         prepare_scratch(row_count, bc_width),
         x_in, cotangent, norm_gain[None, :], w_z, w_x, w_bc, w_dt_padded, *shared,
     )
-    sums = lax.psum(sums, "tensor")
+    (sums,) = pair_sum((sums,), (False,), 1)
     gate_out, y_part, gate_low, x_pre_low, dt_padded, bc_part_grad, partial_grad, rows, heads = (
         local_call(
             functools.partial(backward_kernel, total_width),
@@ -561,11 +619,12 @@
             w_z, w_x, w_dt_padded, *shared,
         )
     )
-    out_share = lax.psum_scatter(y_part, "tensor", scatter_dimension=1, tiled=True)
+    bc_conv_grad, partial_total, out_share = pair_sum(
+        (bc_part_grad, partial_grad, y_part), (False, False, True), 2
+    )
     token_half = lax.dynamic_slice_in_dim(tokens, col_start, half_width, 1)
     result = (token_half + out_share).astype(jnp.bfloat16)
     w_out_grad = lead_contract(cotangent, gate_out)
-    bc_conv_grad = lax.psum(bc_part_grad, "tensor")
     bc_conv_back = jax.vjp(
         lambda *pieces: jax.nn.silu(causal_conv(*pieces)), bc_pre, conv_bc, conv_bc_bias
     )[1]
@@ -574,7 +633,7 @@
     conv_taps = conv_x.shape[0]
     hat_half = lax.dynamic_slice_in_dim(x_hat, col_start, half_width, 1)
     gain_half = lax.dynamic_slice_in_dim(norm_gain, col_start, half_width, 0)
-    normed_grad = lax.psum(partial_grad, "tensor") + tail_contract(bc_pre_low, w_bc)
+    normed_grad = partial_total + tail_contract(bc_pre_low, w_bc)
     grad_half = lax.dynamic_slice_in_dim(normed_grad, col_start, half_width, 1)
     weighted_in = grad_half * gain_half[None, :]
     in_dot = jnp.sum(normed_grad * norm_gain[None, :] * x_hat, axis=1)

time: 228 us -> 184 us (0.81)
  waiting for transfers between devices: 32.7 us -> 0 us
  between operations: 14.1 us -> 1.02 us
  Pallas kernels: 115 us -> 123 us
  local copies, waits for them, and re-layouts: 47.3 us -> 40.5 us
  matrix products: 5.02 us -> 8.31 us
  other arithmetic: 12.3 us -> 9.35 us
    psum x2 -> x0, waiting for transfers between devices: 32.7 us -> none  [the longest x1 21.1 us: on_device(): sums = lax.psum(sums, 'tensor')]
    unnamed x101 -> x77, local copies, waits for them, and re-layouts: 30.8 us -> 22.5 us
    pallas_call x0 -> x2, Pallas kernels: none -> 7.07 us  [pair_sum(): pl.pallas_call(functools.partial(pair_kernel, halved), out_shape=tuple((j...]
  transfers between devices with their start and end apart: 3 -> 0, of which waited for: 2 -> 0; matrix products, arithmetic and copies ran while one was open for 14% -> 0% of each run, Pallas kernels for 38% -> 0%
where the time goes in v1:
time: 184 us; the launch traced here: 183 us
  Pallas kernels  123 us (67%)
  local copies, waits for them, and re-layouts  40.5 us (22%)
  other arithmetic  9.35 us (5%)
  matrix products  8.31 us (5%)
    pallas_call x1, Pallas kernels, reduce_all(): pl.pallas_call(functools.partial(reduce_kernel, bit_orders(levels)), out_...  86.2 us
    pallas_call x2, Pallas kernels, local_call(): pl.pallas_call(body, out_shape=tuple((jax.ShapeDtypeStruct(shape, kind) f...  30.1 us
    unnamed x77, local copies, waits for them, and re-layouts  22.5 us
    pallas_call x2, Pallas kernels, pair_sum(): pl.pallas_call(functools.partial(pair_kernel, halved), out_shape=tuple((j...  7.07 us
    dot_general x4, matrix products, lead_contract(): lax.dot_general(left, right, (((0,), (0,)), ((), ())), preferred_element_...  6.15 us

profile of v1, /device:TPU:0, one launch (start us, length us, event | category | flops | bytes accessed | tf_op | source)
XLA Modules:
  0.0 182.6 jit_solution(482832375874858378)
XLA Ops:
  0.6 0.7 pad_bitcast_fusion
  1.3 0.9 copy.32
  2.3 0.7 broadcast_in_dim.35
  3.1 0.7 broadcast_in_dim.15.cxb_ref
  3.8 0.7 broadcast_in_dim.36.gnorm_ref
  4.5 0.7 broadcast_in_dim.14.gain_ref
  5.2 1.1 copy-done.1
  6.3 1.1 copy-done.6
  7.4 1.3 copy-done.9
  8.7 1.3 copy-done.10
  10.0 1.3 copy-done.11
  11.2 1.0 copy-done.15
  12.2 0.7 copy-done.28
  13.0 0.7 copy-done.30
  13.6 0.7 copy-done.32
  14.3 11.2 %forward.1 = (bf16[512,768]{1,0:T(8,128)(2,1)S(1)}, f32[512,768]{1,0:T(8,128)S(1)}, f32[512,768]{1,0:T(8,128)}, f32[512,256]{1,0:T(8,128)S(1)}, f32[512,128]{1,0...) custom-call(bf16[512,768]{1,0:T(8,128)(2,1)S(1)} %copy-done.1, ...), custom_call_target="tpu_custom_call" | custom-call | tf_op jit(solution)/shard_map/forward/pallas_call | solution.py:317
  25.6 0.9 copy-done.4
  26.4 1.1 copy-done.17
  27.6 1.6 pair_sum.2.sums_ref
  29.2 18.9 %backward.1 = (bf16[512,768]{1,0:T(8,128)(2,1)S(1)}, f32[512,768]{1,0:T(8,128)S(1)}, bf16[512,768]{1,0:T(8,128)(2,1)S(1)}, bf16[512,768]{1,0:T(8,128)(2,1)S(1)},...) custom-call(f32[512,128]{1,0:T(8,128)S(1)} %pair_sum.2.sums_ref, ...), custom_call_target="tpu_custom_call" | custom-call | tf_op jit(solution)/shard_map/backward/pallas_call | solution.py:317
  48.1 0.9 copy-done.12
  49.7 2.0 %copy-done.14 = f32[512,768]{1,0:T(8,128)S(1)} copy-done((f32[512,768]{1,0:T(8,128)S(1)}, f32[512,768]{1,0:T(8,128)}, u32[]{:S(2)}) %copy-start.14) | copy-done | bytes 1572888
  51.7 5.4 %pair_sum.3 = (f32[512,256]{1,0:T(8,128)S(1)}, f32[512,768]{1,0:T(8,128)S(1)}, f32[512,384]{1,0:T(8,128)S(1)}) custom-call(f32[512,256]{1,0:T(8,128)S(1)} %get-tuple-element.49.refs_0_, f32[512,768]{1,0:T(8,128)S(1)} %copy-done.14, f32[512,768]{1,0:T(8,128)S(1)} %get-tuple-element.51.refs_2_), custom_call_target="tpu_custom_call" | custom-call | tf_op jit(solution)/shard_map/pair_sum/pallas_call | solution.py:517
  57.2 1.4 multiply_reduce_fusion.6
  58.7 1.2 broadcast_multiply_fusion.4
  60.1 0.9 copy-done.2
  61.3 2.2 %multiply_reduce_fusion = (f32[512]{0:T(512)S(1)}, f32[512,768]{1,0:T(8,128)}, f32[512,768]{1,0:T(8,128)}) fusion(f32[768]{0:T(1024)S(1)} %copy-done.34, f32[512]{0:T(512)S(1)} %add_rsqrt_fusion, bf16[512,768]{1,0:T(8,128)(2,1)S(1)} %copy-done.2, f32[512,768]{1,0:T(8,128)S(1)} %get-tuple-element.53, bf16[768,256]{1,0:T(8,128)(2,1)S(1)} %copy-done.16, ...), kind=kOutput, calls=%fused_computation.2 | convolution fusion | flops 203685376 | bytes 6168576 | tf_op jit(solution)/shard_map/dot_general | solution.py:24
  63.5 2.4 %multiply_reduce_fusion.2 = (f32[384]{0:T(512)S(1)}, bf16[512,384]{1,0:T(8,128)(2,1)}) fusion(f32[512,768]{1,0:T(8,128)} %get-tuple-element.94, s32[]{:T(128)S(6)} %select_n.2, f32[512,768]{1,0:T(8,128)} %get-tuple-element.107, f32[512]{0:T(512)S(1)} %get-tuple-element.93, f32[384]{0:T(512)S(1)} %dynamic_slice.18, f32[512]{0:T(512)S(1)} %add_rsqrt_fusion, ...), kind=kLoop, calls=%fused_computation.13 | loop fusion | flops 1965696 | bytes 2366468 | tf_op jit(solution)/shard_map/reduce_sum | solution.py:640
  66.7 2.5 %fusion.4 = f32[768,896]{1,0:T(8,128)S(1)} fusion(bf16[512,768]{1,0:T(8,128)(2,1)} %copy-done.4, bf16[512,128]{1,0:T(8,128)(2,1)S(1)} %get-tuple-element.99, bf16[512,768]{1,0:T(8,128)(2,1)} %copy-done.22), kind=kOutput, calls=%fused_computation.9 | convolution fusion | flops 706478080 | bytes 4456448 | tf_op jit(solution)/shard_map/dot_general | solution.py:18
  69.2 2.5 %fusion = f32[768,896]{1,0:T(8,128)} fusion(bf16[512,768]{1,0:T(8,128)(2,1)S(1)} %copy-done.5, bf16[512,128]{1,0:T(8,128)(2,1)S(1)} %get-tuple-element.100, bf16[512,768]{1,0:T(8,128)(2,1)S(1)} %copy-done.21), kind=kOutput, calls=%fused_computation.5 | convolution fusion | flops 706478080 | bytes 4456448 | tf_op jit(solution)/shard_map/dot_general | solution.py:18
  72.1 0.8 copy-done.8
  72.9 0.8 convolution_bitcast_fusion
  73.7 1.7 pad_maximum_fusion
  75.4 3.4 %copy.33 = f32[768,896]{1,0:T(8,128)} copy(f32[768,896]{0,1:T(8,128)} %pad_maximum_fusion) | data formatting | bytes 5505024 | tf_op jit(solution)/shard_map/concatenate | solution.py:651
  78.8 1.8 copy-done
  80.5 1.8 copy-done.3
  82.3 0.8 copy-done.24
  83.1 86.2 %reduce_all.1 = (f32[48,896]{1,0:T(8,128)S(1)}, f32[48,896]{1,0:T(8,128)S(1)}, f32[48,896]{1,0:T(8,128)S(1)}, f32[16,768]{1,0:T(8,128)S(1)}) custom-call(f32[16,48,896]{2,1,0:T(8,128)S(1)} %bitcast.38, f32[16,48,896]{2,1,0:T(8,128)S(1)} %bitcast.37, f32[16,48,896]{2,1,0:T(8,128)S(1)} %bitcast.36, f32[16,768]{1,0:T(8,128)S(1)} %copy-done.24), custom_call_target="tpu_custom_call" | custom-call | tf_op jit(solution)/shard_map/reduce_all/pallas_call | solution.py:452
  170.7 0.7 slice.108
  171.4 0.7 slice_bitcast_fusion
  172.1 0.8 slice.114
  173.5 0.8 reshape.112
  174.8 0.8 slice.117
  176.7 0.7 slice.111
  177.5 0.7 copy.34
  178.1 1.5 slice_reduce_fusion
  180.3 1.3 slice.112
  181.8 0.8 add_convert_fusion.1
  (82 shorter events, 6.8 us)
Async XLA Ops:
  5.2 1.1 copy-start.1
  6.3 1.1 copy-start.6
  7.4 1.3 copy-start.9
  8.7 1.3 copy-start.10
  10.0 1.3 copy-start.11
  11.2 1.0 copy-start.15
  12.2 0.7 copy-start.28
  13.0 0.7 copy-start.30
  13.6 0.7 copy-start.32
  14.3 14.9 %copy-start.29 = (f32[4,768]{1,0:T(4,128)S(1)}, f32[4,768]{1,0:T(4,128)}, u32[]{:S(2)}) copy-start(f32[4,768]{1,0:T(4,128)} %cx_ref.3) | copy-start | bytes 36868
  14.3 14.9 %copy-start.31 = (f32[4,256]{1,0:T(4,128)S(1)}, f32[4,256]{1,0:T(4,128)}, u32[]{:S(2)}) copy-start(f32[4,256]{1,0:T(4,128)} %cbc_ref.3) | copy-start | bytes 12292
  25.6 0.9 copy-start.4
  26.4 1.1 copy-start.17
  48.1 0.9 copy-start.12
  49.0 0.7 copy-start.26
  49.7 7.4 %copy-start.20 = (bf16[512,768]{1,0:T(8,128)(2,1)}, bf16[512,768]{1,0:T(8,128)(2,1)S(1)}, u32[]{:S(2)}) copy-start(bf16[512,768]{1,0:T(8,128)(2,1)S(1)} %get-tuple-element.58) | copy-start | bytes 2359300
  49.7 7.4 %copy-start.22 = (bf16[512,768]{1,0:T(8,128)(2,1)}, bf16[512,768]{1,0:T(8,128)(2,1)S(1)}, u32[]{:S(2)}) copy-start(bf16[512,768]{1,0:T(8,128)(2,1)S(1)} %get-tuple-element.59) | copy-start | bytes 2359300
  49.7 2.0 %copy-start.14 = (f32[512,768]{1,0:T(8,128)S(1)}, f32[512,768]{1,0:T(8,128)}, u32[]{:S(2)}) copy-start(f32[512,768]{1,0:T(8,128)} %get-tuple-element.50.refs_1_) | copy-start | bytes 4718596
  51.7 5.5 %copy-start.33 = (f32[256]{0:T(256)S(1)}, f32[256]{0:T(256)}, u32[]{:S(2)}) copy-start(f32[256]{0:T(256)} %param.26) | copy-start | bytes 3076
  57.1 1.5 copy-start.18
  59.9 1.1 copy-start.2
  59.9 1.4 copy-start.16
  59.9 1.4 copy-start.34
  61.3 2.2 %copy-start.7 = (bf16[512,768]{1,0:T(8,128)(2,1)S(1)}, bf16[512,768]{1,0:T(8,128)(2,1)}, u32[]{:S(2)}) copy-start(bf16[512,768]{1,0:T(8,128)(2,1)} %cot_ref.1) | copy-start | bytes 2359300
  66.6 2.5 %copy-start.5 = (bf16[512,768]{1,0:T(8,128)(2,1)S(1)}, bf16[512,768]{1,0:T(8,128)(2,1)}, u32[]{:S(2)}) copy-start(bf16[512,768]{1,0:T(8,128)(2,1)} %copy-done.4) | copy-start | bytes 2359300
  66.6 2.5 %copy-start.21 = (bf16[512,768]{1,0:T(8,128)(2,1)S(1)}, bf16[512,768]{1,0:T(8,128)(2,1)}, u32[]{:S(2)}) copy-start(bf16[512,768]{1,0:T(8,128)(2,1)} %copy-done.20) | copy-start | bytes 2359300
  69.2 2.6 %copy-start.27 = (bf16[512,128]{1,0:T(8,128)(2,1)S(1)}, bf16[512,128]{1,0:T(8,128)(2,1)}, u32[]{:S(2)}) copy-start(bf16[512,128]{1,0:T(8,128)(2,1)} %copy-done.26) | copy-start | bytes 393220
  69.2 2.9 %copy-start.13 = (bf16[512,768]{1,0:T(8,128)(2,1)S(1)}, bf16[512,768]{1,0:T(8,128)(2,1)}, u32[]{:S(2)}) copy-start(bf16[512,768]{1,0:T(8,128)(2,1)} %copy-done.12) | copy-start | bytes 2359300
  71.7 1.1 copy-start.8
  78.8 1.8 copy-start
  80.5 1.8 copy-start.3
  82.3 0.8 copy-start.24
  169.3 1.4 copy-start.23
  169.3 2.0 %copy-start.25 = (f32[48,896]{1,0:T(8,128)}, f32[48,896]{1,0:T(8,128)S(1)}, u32[]{:S(2)}) copy-start(f32[48,896]{1,0:T(8,128)S(1)} %get-tuple-element.65) | copy-start | bytes 516100
  171.4 10.4 %copy-start.19 = (f32[512,384]{1,0:T(8,128)S(1)}, f32[512,384]{1,0:T(8,128)}, u32[]{:S(2)}) copy-start(f32[512,384]{1,0:T(8,128)} %copy-done.18) | copy-start | bytes 2359300

commit v2 on v1

--- a/solution.py
+++ b/solution.py
@@ -330,17 +330,20 @@
 
 def bit_orders(levels):
     if levels == 4:
-        return ((0, 1, 2, 3), (1, 0, 2, 3), (2, 3, 0, 1))
+        return ((0, 1, 2, 3), (1, 0, 2, 3), (2, 3, 0, 1), (0, 1, 2, 3))
     base = tuple(range(levels))
     third = max(1, levels // 3)
-    return (base, base[third:] + base[:third], base[2 * third :] + base[: 2 * third])
+    return (base, base[third:] + base[:third], base[2 * third :] + base[: 2 * third], base)
 
 
 def reduce_kernel(
-    orders, a_ref, b_ref, c_ref, pack_ref, oa_ref, ob_ref, oc_ref, opack_ref,
-    ra_ref, rb_ref, rc_ref, rpack_ref, spack_ref, send_sem, recv_sem, psend_sem, precv_sem,
+    orders, a_ref, b_ref, c_ref, d_ref, pack_ref,
+    oa_ref, ob_ref, oc_ref, od_ref, obc_ref, opack_ref,
+    ra_ref, rb_ref, rc_ref, rd_ref, rpack_ref, spack_ref, send_sem, recv_sem, psend_sem, precv_sem,
 ):
-    parts, outs, lands = (a_ref, b_ref, c_ref), (oa_ref, ob_ref, oc_ref), (ra_ref, rb_ref, rc_ref)
+    parts, outs = (a_ref, b_ref, c_ref, d_ref), (oa_ref, ob_ref, oc_ref, od_ref)
+    lands = (ra_ref, rb_ref, rc_ref, rd_ref)
+    groups = range(len(parts))
     levels = len(orders[0])
     count = 2**levels
     sizes = [count // 2 ** (stage + 1) for stage in range(levels)]
@@ -394,7 +397,7 @@
     pl.semaphore_wait(barrier, levels)
 
     def begin(k, carry):
-        for g in range(3):
+        for g in groups:
             transfer(g, 0, k).start()
         return carry
 
@@ -402,9 +405,9 @@
     lax.fori_loop(0, sizes[0], begin, 0)
     for stage in range(levels):
         half = sizes[stage] // 2
-        for g in range(3):
-
-            def step(k, carry, g=g, stage=stage, forward=False):
+
+        def step(k, carry, stage=stage, forward=False):
+            for g in groups:
                 transfer(g, stage, k).wait_recv()
                 slot = starts[stage] + k
                 if stage == 0:
@@ -412,19 +415,23 @@
                 else:
                     own = lands[g][starts[stage - 1] + sizes[stage] + k]
                 total = lands[g][slot] + own
-                if stage == levels - 1:
-                    outs[g][...] = total
+                if stage < levels - 1:
+                    lands[g][slot] = total
                 else:
-                    lands[g][slot] = total
+                    main = outs[g].shape[1]
+                    outs[g][...] = total[:, :main]
+                    extra = total.shape[1] - main
+                    if extra:
+                        obc_ref[:, (g - 1) * extra : g * extra] = total[:, main:]
                 if forward:
                     transfer(g, stage + 1, k).start()
-                return carry
-
-            if stage < levels - 1:
-                lax.fori_loop(0, half, functools.partial(step, forward=True), 0)
-                lax.fori_loop(half, sizes[stage], step, 0)
-            else:
-                step(0, 0)
+            return carry
+
+        if stage < levels - 1:
+            lax.fori_loop(0, half, functools.partial(step, forward=True), 0)
+            lax.fori_loop(half, sizes[stage], step, 0)
+        else:
+            step(0, 0)
         pack_transfer(stage).wait_recv()
         before = pack_ref[...] if stage == 0 else spack_ref[stage - 1]
         pack_total = before + rpack_ref[stage]
@@ -437,29 +444,32 @@
         pack_transfer(stage).wait_send()
 
         def finish(k, carry, stage=stage):
-            for g in range(3):
+            for g in groups:
                 transfer(g, stage, k).wait_send()
             return carry
 
         lax.fori_loop(0, sizes[stage], finish, 0)
 
 
-def reduce_all(a, b, c, pack):
+def reduce_all(a, b, c, d, pack):
     count, rows, width = a.shape
     levels = count.bit_length() - 1
     vmem = pl.BlockSpec(memory_space=pltpu.VMEM)
-    part = jax.ShapeDtypeStruct((rows, width), jnp.float32)
+    widths = (width, width, width, d.shape[2], 2 * (b.shape[2] - width))
     return pl.pallas_call(
         functools.partial(reduce_kernel, bit_orders(levels)),
-        out_shape=(part, part, part, jax.ShapeDtypeStruct(pack.shape, jnp.float32)),
-        in_specs=[vmem] * 4,
-        out_specs=(vmem,) * 4,
-        scratch_shapes=[pltpu.VMEM((count - 1, rows, width), jnp.float32)] * 3
+        out_shape=tuple(jax.ShapeDtypeStruct((rows, size), jnp.float32) for size in widths)
+        + (jax.ShapeDtypeStruct(pack.shape, jnp.float32),),
+        in_specs=[vmem] * 5,
+        out_specs=(vmem,) * 6,
+        scratch_shapes=[
+            pltpu.VMEM((count - 1, rows, part.shape[2]), jnp.float32) for part in (a, b, c, d)
+        ]
         + [
             pltpu.VMEM((levels,) + pack.shape, jnp.float32),
             pltpu.VMEM((levels,) + pack.shape, jnp.float32),
-            pltpu.SemaphoreType.DMA((3, count - 1)),
-            pltpu.SemaphoreType.DMA((3, count - 1)),
+            pltpu.SemaphoreType.DMA((4, count - 1)),
+            pltpu.SemaphoreType.DMA((4, count - 1)),
             pltpu.SemaphoreType.DMA((levels,)),
             pltpu.SemaphoreType.DMA((levels,)),
         ],
@@ -467,7 +477,7 @@
             collective_id=0, has_side_effects=True, vmem_limit_bytes=44 * 2**20
         ),
         name="reduce_all",
-    )(a, b, c, pack)
+    )(a, b, c, d, pack)
 
 
 def pair_kernel(halved, *refs):
@@ -648,7 +658,8 @@
     def chunks(array):
         return array.reshape(count, model_width // count, array.shape[1])
 
-    part_a = chunks(jnp.concatenate([w_out_grad, lead_contract(normed, dt_padded)], axis=1))
+    part_a = chunks(w_out_grad)
+    part_d = chunks(lead_contract(normed, dt_padded))
     part_b = chunks(
         lead_contract(normed, jnp.concatenate([gate_low, bc_pre_low[:, :half_bc]], axis=1))
     )
@@ -664,12 +675,11 @@
     )
     flat = jnp.concatenate([array.reshape(-1) for array in small])
     pack = jnp.pad(flat, (0, PACK_ROWS * 768 - flat.shape[0])).reshape(PACK_ROWS, 768)
-    sum_a, sum_b, sum_c, pack_total = reduce_all(part_a, part_b, part_c, pack)
-    w_out_share = jnp.transpose(sum_a[:, :inner_width])
-    w_dt_share = sum_a[:, inner_width : inner_width + heads_here]
-    w_z_share = sum_b[:, :inner_width]
-    w_x_share = sum_c[:, :inner_width]
-    w_bc_share = jnp.concatenate([sum_b[:, inner_width:], sum_c[:, inner_width:]], axis=1)
+    sum_a, w_z_share, w_x_share, sum_d, w_bc_share, pack_total = reduce_all(
+        part_a, part_b, part_c, part_d, pack
+    )
+    w_out_share = jnp.transpose(sum_a)
+    w_dt_share = sum_d[:, :heads_here]
     flat_total = pack_total.reshape(-1)
     totals, at = [], 0
     for array in small:

time: 184 us -> 156 us (0.85)
  local copies, waits for them, and re-layouts: 40.5 us -> 27.7 us
  Pallas kernels: 123 us -> 115 us
  other arithmetic: 9.35 us -> 5.17 us
    pallas_call x1, Pallas kernels: 86.2 us -> 77.7 us  [reduce_all(): pl.pallas_call(functools.partial(reduce_kernel, bit_orders(levels)), out_...]
    concatenate x1 -> x0, local copies, waits for them, and re-layouts: 3.37 us -> none  [on_device(): jnp.concatenate([w_out_grad, lead_contract(normed, dt_padded)], axis=1)]
    unnamed x77 -> x69, local copies, waits for them, and re-layouts: 22.5 us -> 19.3 us
    concatenate x2 -> x0, other arithmetic: 2.36 us -> none  [the longest x1 1.71 us: on_device(): jnp.concatenate([w_out_grad, lead_contract(normed, dt_padded)], axis=1)]
    slice x5 -> x0, local copies, waits for them, and re-layouts: 2.09 us -> none  [the longest x1 0.74 us: on_device(): w_dt_share = sum_a[:, inner_width:inner_width + heads_here]]
where the time goes in v2:
time: 156 us; the launch traced here: 155 us
  Pallas kernels  115 us (74%)
  local copies, waits for them, and re-layouts  27.7 us (18%)
  matrix products  6.66 us (4%)
  other arithmetic  5.17 us (3%)
    pallas_call x1, Pallas kernels, reduce_all(): pl.pallas_call(functools.partial(reduce_kernel, bit_orders(levels)), out_...  77.7 us
    pallas_call x2, Pallas kernels, local_call(): pl.pallas_call(body, out_shape=tuple((jax.ShapeDtypeStruct(shape, kind) f...  30 us
    unnamed x69, local copies, waits for them, and re-layouts  19.3 us
    pallas_call x2, Pallas kernels, pair_sum(): pl.pallas_call(functools.partial(pair_kernel, halved), out_shape=tuple((j...  7.08 us
    dot_general x4, matrix products, lead_contract(): lax.dot_general(left, right, (((0,), (0,)), ((), ())), preferred_element_...  4.46 us

profile of v2, /device:TPU:0, one launch (start us, length us, event | category | flops | bytes accessed | tf_op | source)
XLA Modules:
  0.0 155.3 jit_solution(11709061429327158873)
XLA Ops:
  0.6 0.7 pad_bitcast_fusion
  1.3 0.9 copy.32
  2.3 0.7 broadcast_in_dim.35
  3.1 0.7 broadcast_in_dim.15.cxb_ref
  3.8 0.7 broadcast_in_dim.36.gnorm_ref
  4.5 0.7 broadcast_in_dim.14.gain_ref
  5.2 1.1 copy-done
  6.3 1.1 copy-done.2
  7.4 1.3 copy-done.4
  8.7 1.3 copy-done.6
  10.0 1.3 copy-done.8
  11.2 1.0 copy-done.11
  12.2 0.7 copy-done.21
  13.0 0.7 copy-done.23
  13.6 0.7 copy-done.25
  14.3 11.2 %forward.1 = (bf16[512,768]{1,0:T(8,128)(2,1)S(1)}, f32[512,768]{1,0:T(8,128)S(1)}, f32[512,768]{1,0:T(8,128)}, f32[512,256]{1,0:T(8,128)S(1)}, f32[512,128]{1,0...) custom-call(bf16[512,768]{1,0:T(8,128)(2,1)S(1)} %copy-done, ...), custom_call_target="tpu_custom_call" | custom-call | tf_op jit(solution)/shard_map/forward/pallas_call | solution.py:317
  25.5 1.1 copy-done.15
  26.7 1.6 %pair_sum.2.sums_ref = f32[512,128]{1,0:T(8,128)S(1)} custom-call(f32[512,128]{1,0:T(8,128)S(1)} %get-tuple-element.43.refs_0_), custom_call_target="tpu_custom_call" | custom-call | tf_op jit(solution)/shard_map/pair_sum/pallas_call | solution.py:527
  28.4 18.8 %backward.1 = (bf16[512,768]{1,0:T(8,128)(2,1)S(1)}, f32[512,768]{1,0:T(8,128)S(1)}, bf16[512,768]{1,0:T(8,128)(2,1)S(1)}, bf16[512,768]{1,0:T(8,128)(2,1)S(1)},...) custom-call(f32[512,128]{1,0:T(8,128)S(1)} %pair_sum.2.sums_ref, ...), custom_call_target="tpu_custom_call" | custom-call | tf_op jit(solution)/shard_map/backward/pallas_call | solution.py:317
  47.2 2.0 %copy-done.10 = f32[512,768]{1,0:T(8,128)S(1)} copy-done((f32[512,768]{1,0:T(8,128)S(1)}, f32[512,768]{1,0:T(8,128)}, u32[]{:S(2)}) %copy-start.10) | copy-done | bytes 1572888
  49.2 5.4 %pair_sum.3 = (f32[512,256]{1,0:T(8,128)S(1)}, f32[512,768]{1,0:T(8,128)S(1)}, f32[512,384]{1,0:T(8,128)S(1)}) custom-call(f32[512,256]{1,0:T(8,128)S(1)} %get-tuple-element.51.refs_0_, f32[512,768]{1,0:T(8,128)S(1)} %copy-done.10, f32[512,768]{1,0:T(8,128)S(1)} %get-tuple-element.53.refs_2_), custom_call_target="tpu_custom_call" | custom-call | tf_op jit(solution)/shard_map/pair_sum/pallas_call | solution.py:527
  54.7 0.9 copy-done.16
  55.6 0.6 multiply_reduce_fusion.6
  56.2 0.5 copy-done.13
  57.2 0.9 copy-done.1
  58.1 0.2 multiply_reduce_fusion.1
  58.3 0.5 copy-done.14
  58.8 2.2 %multiply_reduce_fusion = (f32[512]{0:T(512)S(1)}, f32[512,768]{1,0:T(8,128)}, f32[512,768]{1,0:T(8,128)}) fusion(f32[768]{0:T(1024)S(1)} %copy-done.28, f32[512]{0:T(512)S(1)} %add_rsqrt_fusion, bf16[512,768]{1,0:T(8,128)(2,1)S(1)} %copy-done.1, f32[512,768]{1,0:T(8,128)S(1)} %copy-done.14, bf16[768,256]{1,0:T(8,128)(2,1)S(1)} %copy-done.12, ...), kind=kOutput, calls=%fused_computation | convolution fusion | flops 203685376 | bytes 6168576 | tf_op jit(solution)/shard_map/dot_general | solution.py:24
  61.1 2.4 %multiply_reduce_fusion.2 = (f32[384]{0:T(512)S(1)}, bf16[512,384]{1,0:T(8,128)(2,1)}) fusion(f32[512,768]{1,0:T(8,128)} %get-tuple-element.98, s32[]{:T(128)S(6)} %select_n.2, f32[512,768]{1,0:T(8,128)} %get-tuple-element.111, f32[512]{0:T(512)S(1)} %get-tuple-element.97, f32[384]{0:T(512)S(1)} %dynamic_slice.18, f32[512]{0:T(512)S(1)} %add_rsqrt_fusion, ...), kind=kLoop, calls=%fused_computation.11 | loop fusion | flops 1965696 | bytes 2366468 | tf_op jit(solution)/shard_map/reduce_sum | solution.py:650
  63.6 1.0 fusion.14
  64.6 2.2 %fusion.4 = f32[768,896]{1,0:T(8,128)S(1)} fusion(bf16[512,768]{1,0:T(8,128)(2,1)S(1)} %get-tuple-element.58, bf16[512,128]{1,0:T(8,128)(2,1)S(1)} %get-tuple-element.103, bf16[512,768]{1,0:T(8,128)(2,1)} %copy-done.20), kind=kOutput, calls=%fused_computation.7 | convolution fusion | flops 706478080 | bytes 4456448 | tf_op jit(solution)/shard_map/dot_general | solution.py:18
  66.9 1.0 fusion
  67.9 0.4 fusion.17
  68.3 0.8 fusion.16
  69.1 77.7 %reduce_all.1 = (f32[48,768]{1,0:T(8,128)S(1)}, f32[48,768]{1,0:T(8,128)S(1)}, f32[48,768]{1,0:T(8,128)S(1)}, f32[48,128]{1,0:T(8,128)S(1)}, f32[48,256]{1,0:T(8,128)S(1)}, /*index=5*/f32[16,768]{1,0:T(8,128)S(1)}) custom-call(f32[16,48,768]{2,1,0:T(8,128)S(1)} %bitcast.37, f32[16,48,896]{2,1,0:T(8,128)S(1)} %bitcast.39, f32[16,48,896]{2,1,0:T(8,128)S(1)} %bitcast.38, ...), custom_call_target="tpu_custom_call" | custom-call | tf_op jit(solution)/shard_map/reduce_all/pallas_call | solution.py:459
  146.9 0.6 slice.106
  147.5 0.6 slice.105
  148.1 0.5 slice_bitcast_fusion
  148.6 0.6 slice.107
  149.2 0.6 slice_reduce_fusion
  149.8 0.6 reduce_sum.92
  150.5 0.6 slice.93
  151.1 0.7 copy.33
  151.9 0.8 add_convert_fusion.1
  152.7 0.7 copy.43
  153.4 0.7 copy.44
  154.0 0.6 copy.45
  154.6 0.7 copy.46
  (65 shorter events, 0.9 us)
Async XLA Ops:
  5.2 1.1 copy-start
  6.3 1.1 copy-start.2
  7.4 1.3 copy-start.4
  8.7 1.3 copy-start.6
  10.0 1.3 copy-start.8
  11.2 1.0 copy-start.11
  12.2 0.7 copy-start.21
  12.9 0.7 copy-start.23
  13.6 0.7 copy-start.25
  14.3 14.0 %copy-start.5 = (bf16[768,768]{1,0:T(8,128)(2,1)S(1)}, bf16[768,768]{1,0:T(8,128)(2,1)}, u32[]{:S(2)}) copy-start(bf16[768,768]{1,0:T(8,128)(2,1)} %wz_ref.3) | copy-start | bytes 3538948
  14.3 14.0 %copy-start.7 = (bf16[768,768]{1,0:T(8,128)(2,1)S(1)}, bf16[768,768]{1,0:T(8,128)(2,1)}, u32[]{:S(2)}) copy-start(bf16[768,768]{1,0:T(8,128)(2,1)} %wx_ref.3) | copy-start | bytes 3538948
  14.3 14.0 %copy-start.9 = (bf16[768,768]{1,0:T(8,128)(2,1)S(1)}, bf16[768,768]{1,0:T(8,128)(2,1)}, u32[]{:S(2)}) copy-start(bf16[768,768]{1,0:T(8,128)(2,1)} %wout_ref.3) | copy-start | bytes 3538948
  14.3 14.0 %copy-start.22 = (f32[4,768]{1,0:T(4,128)S(1)}, f32[4,768]{1,0:T(4,128)}, u32[]{:S(2)}) copy-start(f32[4,768]{1,0:T(4,128)} %cx_ref.3) | copy-start | bytes 36868
  14.3 14.0 %copy-start.24 = (f32[4,256]{1,0:T(4,128)S(1)}, f32[4,256]{1,0:T(4,128)}, u32[]{:S(2)}) copy-start(f32[4,256]{1,0:T(4,128)} %cbc_ref.3) | copy-start | bytes 12292
  14.3 14.0 %copy-start.26 = (f32[256]{0:T(256)S(1)}, f32[256]{0:T(256)}, u32[]{:S(2)}) copy-start(f32[256]{0:T(256)} %param.26) | copy-start | bytes 3076
  25.5 1.1 copy-start.15
  47.2 7.4 %copy-start.18 = (bf16[512,768]{1,0:T(8,128)(2,1)}, bf16[512,768]{1,0:T(8,128)(2,1)S(1)}, u32[]{:S(2)}) copy-start(bf16[512,768]{1,0:T(8,128)(2,1)S(1)} %get-tuple-element.59) | copy-start | bytes 2359300
  47.2 7.4 %copy-start.20 = (bf16[512,768]{1,0:T(8,128)(2,1)}, bf16[512,768]{1,0:T(8,128)(2,1)S(1)}, u32[]{:S(2)}) copy-start(bf16[512,768]{1,0:T(8,128)(2,1)S(1)} %get-tuple-element.60) | copy-start | bytes 2359300
  47.2 2.0 %copy-start.10 = (f32[512,768]{1,0:T(8,128)S(1)}, f32[512,768]{1,0:T(8,128)}, u32[]{:S(2)}) copy-start(f32[512,768]{1,0:T(8,128)} %get-tuple-element.52.refs_1_) | copy-start | bytes 4718596
  54.7 0.9 copy-start.16
  55.6 1.2 copy-start.13
  57.0 1.1 copy-start.1
  57.0 1.4 copy-start.12
  57.0 1.9 %copy-start.14 = (f32[512,768]{1,0:T(8,128)S(1)}, f32[512,768]{1,0:T(8,128)}, u32[]{:S(2)}) copy-start(f32[512,768]{1,0:T(8,128)} %copy-done.13) | copy-start | bytes 4718596
  57.0 1.8 %copy-start.28 = (f32[768]{0:T(1024)S(1)}, f32[768]{0:T(1024)}, u32[]{:S(2)}) copy-start(f32[768]{0:T(1024)} %param.18) | copy-start | bytes 9220
  57.2 3.9 %copy-start.27 = (bf16[515,256]{1,0:T(8,128)(2,1)}, bf16[515,256]{1,0:T(8,128)(2,1)S(1)}, u32[]{:S(2)}) copy-start(bf16[515,256]{1,0:T(8,128)(2,1)S(1)} %add_convert_fusion.2) | copy-start | bytes 791044
  58.8 2.3 %copy-start.3 = (bf16[512,768]{1,0:T(8,128)(2,1)S(1)}, bf16[512,768]{1,0:T(8,128)(2,1)}, u32[]{:S(2)}) copy-start(bf16[512,768]{1,0:T(8,128)(2,1)} %cot_ref.1) | copy-start | bytes 2359300
  64.6 2.2 %copy-start.19 = (bf16[512,768]{1,0:T(8,128)(2,1)S(1)}, bf16[512,768]{1,0:T(8,128)(2,1)}, u32[]{:S(2)}) copy-start(bf16[512,768]{1,0:T(8,128)(2,1)} %copy-done.18) | copy-start | bytes 2359300
  146.8 5.0 %copy-start.17 = (f32[512,384]{1,0:T(8,128)S(1)}, f32[512,384]{1,0:T(8,128)}, u32[]{:S(2)}) copy-start(f32[512,384]{1,0:T(8,128)} %copy-done.16) | copy-start | bytes 2359300
